TPU v7x, 256 devices: a whole 4x4x8 slice. The times are simulated.
256 devices in a mesh: rep: 16 (over y, z_lo, core), exp: 16 (over x, z_hi).
Axes of the slice: x: 4, y: 4, z: 8 (z_hi: 4, z_lo: 2; z = z_hi * 2 + z_lo), core: 2. Of those that a mesh axis runs over, the one named last changes fastest.
Arguments:
- tokens: bfloat16 [32768, 1440], P(('rep', 'exp')), may hold values from -6 to 6
- expert_ids: int32 [32768, 4], P(('rep', 'exp')), may hold values from 0 to 127, all different within a row; in each aligned block of 128 rows (0 to 127, 128 to 255, ...) at most 5 rows name the same one
- route_weights: float32 [32768, 4], P(('rep', 'exp')), may hold values from 0.05 to 1
- w_in: bfloat16 [16, 16, 1440, 1440], P('rep', 'exp'), may hold values from -0.15625 to 0.15625
- w_down: bfloat16 [16, 16, 720, 1440], P('rep', 'exp'), may hold values from -0.15625 to 0.15625
- spare_source: int32 [2], replicated, may hold values from 0 to 7, as said below
- spare_host: int32 [2], replicated, may hold values from 8 to 15, as said below
Outputs:
- mixed: bfloat16 [32768, 1440], P(('rep', 'exp'))
- slot_load: int32 [16, 16], P('rep', 'exp')
Inputs may be any that keep to these rules, and one draw needn't show every extreme that they name: `expert_ids`: in the 128 rows of one device no expert is named more than 5 times, a bound that some block reaches. `spare_source`: 2 different exp indices of the lower half of the exp axis. `spare_host`: 2 different exp indices of the upper half of the exp axis.
All inputs are finite; a program needn't handle non-finite values.
Results may differ from a plain program's by a relative error of at most 0.0058.
Values may be sent and summed in bfloat16 or wider, within the bound.
A program may use at most 128 MiB of HBM per device.

v0:
```python
import jax
import jax.numpy as jnp
from jax import lax
from jax.experimental import pallas as pl
from jax.experimental.pallas import tpu as pltpu
from jax.sharding import PartitionSpec as P

MESH = pl.DeviceIdType.MESH
F32 = jnp.float32
BF16 = jnp.bfloat16

NX, NY, NZ = 4, 4, 8
NSRC = 2 * NZ
CAP = 5
UNIT = NSRC * CAP
ROWS = NX * 2 * UNIT
CODE = 1024
CHUNKS = ((0, 512), (512, 1024), (1024, 1440))
NC = len(CHUNKS)
OFFS = (0, -1, 1, -2, 2, -3, 3, 4)


def device(x, y, z, k):
    return (y * 4 + lax.rem(z, 2) * 2 + k, x * 4 + lax.div(z, 2))


def moe_kernel(ids_ref, wts_ref, tok_ref, wi_hbm, wd_hbm, out_ref, *scratch):
    T, G, XY, PP, RY, SS, RX, ZC, ZR = (scratch[i * NC:(i + 1) * NC] for i in range(9))
    meta, OH, CT, WI, WU, WD, send_sems, recv_sems, meta_send, meta_recv, load_sems = scratch[9 * NC:]
    tok_rows = tok_ref.shape[0]
    half = tok_rows // 2
    ff = WD.shape[0]

    rep, ex = lax.axis_index("rep"), lax.axis_index("exp")
    y, k = lax.div(rep, 4), lax.rem(rep, 2)
    x = lax.div(ex, 4)
    z = lax.rem(ex, 4) * 2 + lax.rem(lax.div(rep, 2), 2)
    me = z * 2 + k
    p = lax.rem(y, 2)

    def zat(d):
        return lax.rem(z + d + NZ, NZ)

    def yat(d):
        return lax.rem(y + d + NY, NY)

    def xat(d):
        return lax.rem(x + d + NX, NX)

    ids_of = {}
    sends = []

    def sem_of(name):
        if name not in ids_of:
            ids_of[name] = len(ids_of)
        return ids_of[name]

    def send(name, src, dst, to):
        i = sem_of(name)
        copy = pltpu.make_async_remote_copy(
            src_ref=src, dst_ref=dst, send_sem=send_sems.at[i], recv_sem=recv_sems.at[i],
            device_id=to, device_id_type=MESH)
        copy.start()
        sends.append(copy)

    def arrived(name, dst):
        i = sem_of(name)
        pltpu.make_async_remote_copy(
            src_ref=dst, dst_ref=dst, send_sem=send_sems.at[i], recv_sem=recv_sems.at[i],
            device_id=device(x, y, z, 1 - k), device_id_type=MESH).wait_recv()

    def drain():
        for copy in sends:
            copy.wait_send()
        sends.clear()

    barrier = pltpu.get_barrier_semaphore()
    for j in range(1, NSRC):
        peer = lax.rem(me + j, NSRC)
        pl.semaphore_signal(barrier, inc=1, device_id=device(x, y, lax.div(peer, 2), lax.rem(peer, 2)), device_id_type=MESH)
    for j in range(1, NX):
        pl.semaphore_signal(barrier, inc=1, device_id=device(xat(j), y, z, k), device_id_type=MESH)
    for j in range(1, NY):
        pl.semaphore_signal(barrier, inc=1, device_id=device(x, yat(j), z, k), device_id_type=MESH)

    load_in = pltpu.make_async_copy(wi_hbm, WI, load_sems.at[0])
    load_down = pltpu.make_async_copy(wd_hbm, WD, load_sems.at[1])
    load_in.start()
    load_down.start()
    for c, (lo, hi) in enumerate(CHUNKS):
        T[c][me] = tok_ref[:, lo:hi]
    pl.semaphore_wait(barrier, NSRC - 1 + NX - 1 + NY - 1)

    def block(c, d, rows=None, core=None):
        ref = T[c].at[zat(d) * 2 + (k if core is None else core)]
        return ref if rows is None else ref.at[pl.ds(rows, half)]

    def to_sibling(c, d):
        send(("sib", c, d), block(c, d), block(c, d), device(x, y, z, 1 - k))

    def gather_step(c, s):
        if s == 1:
            to_send = ((1, block(c, 0)), (-1, block(c, 0)))
        else:
            for way in (1, -1):
                rows = None if s <= 4 else (0 if way == 1 else half)
                arrived(("ag", c, s - 1, way), block(c, -(s - 1) * way, rows))
            to_send = ()
            if s <= 4:
                to_send = tuple(
                    (way, block(c, -(s - 1) * way, None if s < 4 else (0 if way == 1 else half))) for way in (1, -1))
        for way, ref in to_send:
            send(("ag", c, s, way), ref, ref, device(x, y, zat(way), k))
        if s == 1:
            to_sibling(c, 0)
        elif s <= 4:
            to_sibling(c, -(s - 1))
            to_sibling(c, s - 1)
        else:
            to_sibling(c, 4)

    def make_meta():
        experts = lax.broadcasted_iota(jnp.int32, (tok_rows, 128), 1)
        total = jnp.zeros((tok_rows, 128), F32)
        hits = []
        for i in range(4):
            hit = (ids_ref[:, i:i + 1] == experts).astype(F32)
            hits.append(hit)
            total = total + hit
        before = (lax.broadcasted_iota(jnp.int32, (tok_rows, tok_rows), 0)
                  > lax.broadcasted_iota(jnp.int32, (tok_rows, tok_rows), 1)).astype(BF16)
        earlier = jnp.dot(before, total.astype(BF16), preferred_element_type=F32)
        table = jnp.zeros((tok_rows, 128), F32)
        for i in range(4):
            rank = jnp.sum(earlier * hits[i], axis=1, keepdims=True)
            e = ids_ref[:, i:i + 1]
            owner = ((e >> 3) & 3) * 4 + ((e >> 1) & 1) * 2 + (e & 1)
            place = ((e >> 5) * 2 + ((e >> 2) & 1)) * UNIT
            code = (owner * CODE + place).astype(F32) + rank
            table = jnp.where(experts == i, code, table)
            table = jnp.where(experts == 4 + i, wts_ref[:, i:i + 1], table)
        meta[me] = table.T[0:8, :]

    def send_meta():
        def one(j, carry):
            peer = lax.rem(me + j, NSRC)
            pltpu.make_async_remote_copy(
                src_ref=meta.at[me], dst_ref=meta.at[me], send_sem=meta_send.at[j], recv_sem=meta_recv.at[j],
                device_id=device(x, y, lax.div(peer, 2), lax.rem(peer, 2)), device_id_type=MESH).start()
            return carry
        lax.fori_loop(1, NSRC, one, 0)

    def meta_copy(j):
        peer = lax.rem(me + NSRC - j, NSRC)
        return pltpu.make_async_remote_copy(
            src_ref=meta.at[peer], dst_ref=meta.at[peer], send_sem=meta_send.at[j], recv_sem=meta_recv.at[j],
            device_id=device(x, y, lax.div(peer, 2), lax.rem(peer, 2)), device_id_type=MESH)

    def build_pick():
        def wait_one(j, carry):
            meta_copy(j).wait_recv()
            return carry
        lax.fori_loop(1, NSRC, wait_one, 0)

        def one(s, carry):
            row = lax.broadcasted_iota(jnp.int32, (ROWS, tok_rows), 0).astype(F32)
            shift = (s * CAP - me * CODE).astype(F32)
            codes = meta[s] + shift
            hit = row == codes[0:1, :]
            for i in range(1, 4):
                hit = jnp.logical_or(hit, row == codes[i:i + 1, :])
            OH[:, pl.ds(pl.multiple_of(s * tok_rows, tok_rows), tok_rows)] = jnp.where(hit, 1.0, 0.0).astype(BF16)
            return carry
        lax.fori_loop(0, NSRC, one, 0)

    def build_combine():
        def one(s, carry):
            col = lax.broadcasted_iota(jnp.int32, (tok_rows, ROWS), 1).astype(F32)
            shift = (s * CAP - me * CODE).astype(F32)
            info = meta[s].T
            total = jnp.zeros((tok_rows, ROWS), F32)
            for i in range(4):
                total = jnp.where(col == info[:, i:i + 1] + shift, info[:, 4 + i:5 + i], total)
            CT[pl.ds(pl.multiple_of(s * tok_rows, tok_rows), tok_rows), :] = total.astype(BF16)
            return carry
        lax.fori_loop(0, NSRC, one, 0)

    def x_stage(c):
        width = CHUNKS[c][1] - CHUNKS[c][0]
        for d in OFFS:
            arrived(("sib", c, d), block(c, d, core=1 - k))
        for j in (2, 1, 3, 0):
            xp = xat(j)
            picked = jnp.dot(
                OH[pl.ds(pl.multiple_of(xp * 2 * UNIT, 2 * UNIT), 2 * UNIT), :],
                T[c][...].reshape(NSRC * tok_rows, width),
                preferred_element_type=F32).astype(BF16).reshape(2, UNIT, width)
            if j == 0:
                XY[c][0, x] = picked[0]
                XY[c][1, x] = picked[1]
            else:
                G[c][j - 1] = picked
                send(("x", c, j), G[c].at[j - 1], XY[c].at[pl.ds(0, 2), x], device(xp, y, z, k))

    def y_stage(c):
        for j in (1, 3, 2):
            arrived(("x", c, j), XY[c].at[pl.ds(0, 2), xat(-j)])
        for j in (1, 3, 2):
            a = lax.rem(p + j, 2)
            send(("y", c, j), XY[c].at[a], XY[c].at[1 + j], device(x, yat(j), z, k))

    def load_weights():
        load_in.wait()
        load_down.wait()

        def one(i, carry):
            rows = pl.ds(pl.multiple_of(i * 160, 16), 160)
            WU[rows, :] = WI[rows, ff:2 * ff]
            return carry
        lax.fori_loop(0, WI.shape[0] // 160, one, 0)

    def expert(j):
        slot = p if j == 0 else 1 + j
        if j:
            for c in range(NC):
                arrived(("y", c, j), XY[c].at[slot])

        def one(q, carry):
            gate = up = None
            for c, (lo, hi) in enumerate(CHUNKS):
                rows = XY[c][slot, pl.ds(q * 2, 2)].reshape(2 * UNIT, hi - lo)
                g = jnp.dot(rows, WI[lo:hi, 0:ff], preferred_element_type=F32)
                u = jnp.dot(rows, WU[lo:hi, :], preferred_element_type=F32)
                gate, up = (g, u) if gate is None else (gate + g, up + u)
            hidden = ((up + 1.0) * gate * jax.nn.sigmoid(1.702 * gate)).astype(BF16)
            for c, (lo, hi) in enumerate(CHUNKS):
                part = jnp.dot(hidden, WD[:, lo:hi], preferred_element_type=F32).astype(BF16)
                PP[c][j, pl.ds(q * 2, 2)] = part.reshape(2, UNIT, hi - lo)
            return carry
        lax.fori_loop(0, 2, one, 0)
        if j:
            for c in range(NC):
                send(("ry", c, j), PP[c].at[j], RY[c].at[j - 1], device(x, yat(-j), z, k))

    def halves(c, odd):
        if odd:
            arrived(("ry", c, 1), RY[c].at[0])
            arrived(("ry", c, 3), RY[c].at[2])
            first, second = RY[c].at[0], RY[c].at[2]
        else:
            arrived(("ry", c, 2), RY[c].at[1])
            first, second = PP[c].at[0], RY[c].at[1]
        a = lax.rem(p + odd, 2)

        def one(i, carry):
            SS[c][odd, i] = (first[i].astype(F32) + second[i].astype(F32)).astype(BF16)
            return carry
        lax.fori_loop(0, NX, one, 0)
        for j in (2, 1, 3):
            xs = xat(j)
            send(("rx", c, odd, j), SS[c].at[odd, xs], RX[c].at[x, a], device(xs, y, z, k))
        RX[c][x, a] = SS[c][odd, x]

    def combined(c, s):
        width = CHUNKS[c][1] - CHUNKS[c][0]
        return jnp.dot(
            CT[pl.ds(pl.multiple_of(s * tok_rows, tok_rows), tok_rows), :],
            RX[c][...].reshape(ROWS, width), preferred_element_type=F32)

    def combine_sibling(c):
        for odd in (1, 0):
            a = lax.rem(p + odd, 2)
            for j in (2, 1, 3):
                arrived(("rx", c, odd, j), RX[c].at[xat(-j), a])
        for d in OFFS[::-1]:
            s = zat(d) * 2 + 1 - k
            T[c][s] = combined(c, s).astype(BF16)
            send(("zc", c, d), T[c].at[s], ZC[c].at[zat(d)], device(x, y, z, 1 - k))

    def scatter_step(c, s):
        lo, hi = CHUNKS[c]
        if s == 0:
            arrived(("zc", c, 4), ZC[c].at[zat(4)])
            own = T[c].at[zat(4) * 2 + k]
            own[...] = (combined(c, zat(4) * 2 + k) + ZC[c][zat(4)].astype(F32)).astype(BF16)
            for i, way in enumerate((1, -1)):
                rows = pl.ds(i * half, half)
                send(("rs", c, 0, way), own.at[rows], ZR[c].at[i * 4, rows], device(x, y, zat(way), k))
        elif s < 4:
            for i, way in enumerate((1, -1)):
                d = way * (4 - s)
                arrived(("zc", c, d), ZC[c].at[zat(d)])
                total = combined(c, zat(d) * 2 + k) + ZC[c][zat(d)].astype(F32)
                own = T[c].at[zat(d) * 2 + k]
                if s == 1:
                    rows = pl.ds(i * half, half)
                    arrived(("rs", c, 0, way), ZR[c].at[i * 4, rows])
                    mine = total[i * half:(i + 1) * half] + ZR[c][i * 4, rows].astype(F32)
                    own[rows, :] = mine.astype(BF16)
                    other = 1 - i
                    own[pl.ds(other * half, half), :] = total[other * half:(other + 1) * half].astype(BF16)
                else:
                    arrived(("rs", c, s - 1, way), ZR[c].at[i * 4 + s - 1])
                    own[...] = (total + ZR[c][i * 4 + s - 1].astype(F32)).astype(BF16)
                send(("rs", c, s, way), own, ZR[c].at[i * 4 + s], device(x, y, zat(way), k))
        else:
            arrived(("zc", c, 0), ZC[c].at[z])
            total = combined(c, me) + ZC[c][z].astype(F32)
            for i, way in enumerate((1, -1)):
                arrived(("rs", c, 3, way), ZR[c].at[i * 4 + 3])
                total = total + ZR[c][i * 4 + 3].astype(F32)
            out_ref[:, lo:hi] = total.astype(BF16)

    gather_step(0, 1)
    make_meta()
    send_meta()
    for t in range(2, 5 + 2 * NC):
        for c in range(NC):
            s = t - 2 * c
            if 1 <= s <= 5 and (c, s) != (0, 1):
                gather_step(c, s)
        if t == 3:
            build_pick()
        for c in range(NC):
            if t - 2 * c == 5:
                x_stage(c)
                if c:
                    y_stage(c - 1)
        if t == 6:
            load_weights()
    y_stage(NC - 1)
    expert(0)
    drain()
    build_combine()
    for j in (1, 3, 2):
        expert(j)
        if j == 3:
            for c in range(NC):
                halves(c, 1)
    for c in range(NC):
        halves(c, 0)
    order = sorted((s + 2 * c, -c, c, s) for c in range(NC) for s in range(5))
    started = set()
    for _, _, c, s in order:
        if c not in started:
            started.add(c)
            combine_sibling(c)
        scatter_step(c, s)
    drain()

    def end_one(j, carry):
        meta_copy(j).wait_send()
        return carry
    lax.fori_loop(1, NSRC, end_one, 0)
    assert len(ids_of) <= send_sems.shape[0]


def moe(ids, weights, tokens, w_in, w_down):
    rows, model = tokens.shape
    widths = [hi - lo for lo, hi in CHUNKS]
    lead = (
        (NSRC, rows), (3, 2, UNIT), (5, NX, UNIT), (4, NX, UNIT), (3, NX, UNIT), (2, NX, UNIT), (NX, 2, UNIT),
        (NZ, rows), (8, rows))
    buffers = [pltpu.VMEM(shape + (width,), BF16) for shape in lead for width in widths]
    copies = NC * (8 + 8 + 3 + 3 + 3 + 6 + 8 + 8)
    vmem = pl.BlockSpec(memory_space=pltpu.VMEM)
    hbm = pl.BlockSpec(memory_space=pl.ANY)
    return pl.pallas_call(
        moe_kernel,
        out_shape=jax.ShapeDtypeStruct((rows, model), BF16),
        in_specs=[vmem, vmem, vmem, hbm, hbm],
        out_specs=vmem,
        scratch_shapes=buffers + [
            pltpu.VMEM((NSRC, 8, 128), F32),
            pltpu.VMEM((ROWS, NSRC * rows), BF16),
            pltpu.VMEM((NSRC * rows, ROWS), BF16),
            pltpu.VMEM(w_in.shape, BF16),
            pltpu.VMEM((w_in.shape[0], w_down.shape[0]), BF16),
            pltpu.VMEM(w_down.shape, BF16),
            pltpu.SemaphoreType.DMA((copies,)),
            pltpu.SemaphoreType.DMA((copies,)),
            pltpu.SemaphoreType.DMA((NSRC,)),
            pltpu.SemaphoreType.DMA((NSRC,)),
            pltpu.SemaphoreType.DMA((2,)),
        ],
        compiler_params=pltpu.CompilerParams(
            collective_id=0, has_side_effects=True, vmem_limit_bytes=60 * 1024 * 1024),
        cost_estimate=pl.CostEstimate(flops=16 * 10**9, bytes_accessed=7 * 10**6, transcendentals=10**6),
    )(ids, weights, tokens, w_in, w_down)


def local(tokens, expert_ids, route_weights, w_in, w_down, spare_source, spare_host):
    rep_count = lax.axis_size("rep")
    column_count = lax.axis_size("exp")
    group_count = rep_count // 2
    expert_count = group_count * column_count
    rep, column = lax.axis_index("rep"), lax.axis_index("exp")

    experts = jnp.arange(expert_count, dtype=jnp.int32)
    counts = jnp.sum((expert_ids.reshape(-1)[:, None] == experts[None, :]).astype(jnp.int32), axis=0)
    upper = jnp.where(rep >= group_count, counts, 0)
    both = lax.psum(jnp.stack([counts, upper]), ("rep", "exp"))

    mixed = moe(expert_ids, route_weights, tokens, w_in[0, 0], w_down[0, 0])

    residue = rep % group_count
    own = column * group_count + residue
    is_source = jnp.any(column == spare_source)
    load = jnp.take(both[0], own) - jnp.where(is_source, jnp.take(both[1], own), 0)
    copied = jnp.take(both[1], spare_source * group_count + residue)
    load = load + jnp.sum(jnp.where(column == spare_host, copied, 0))
    return mixed, load.astype(jnp.int32).reshape(1, 1)


def solution(mesh):
    placed = (
        P(("rep", "exp"), None),
        P(("rep", "exp"), None),
        P(("rep", "exp"), None),
        P("rep", "exp", None, None),
        P("rep", "exp", None, None),
        P(),
        P(),
    )
    return jax.shard_map(
        local,
        mesh=mesh,
        in_specs=placed,
        out_specs=(P(("rep", "exp"), None), P("rep", "exp")),
        check_vma=False,
    )
```

profile of v0, /device:TPU:32, one launch (start us, length us, event | category | flops | bytes accessed | tf_op | source)
XLA Modules:
  0.0 275.6 jit_solution(9323600976358182755)
XLA Ops:
  0.6 1.4 copy.18.ids_ref
  2.0 1.4 copy.19.wts_ref
  3.4 1.9 copy.20.tok_ref
  5.3 0.0 copy-start
  5.3 0.0 copy-start.1
  5.3 0.0 copy-start.2
  5.4 185.3 %shard_map.86 = bf16[128,1440]{1,0:T(8,128)(2,1)} custom-call(s32[128,4]{1,0:T(8,128)} %copy.18.ids_ref, f32[128,4]{1,0:T(8,128)} %copy.19.wts_ref, bf16[128,1440]{1,0:T(8,128)(2,1)} %copy.20.tok_ref, bf16[1440,1440]{1,0:T(8,128)(2,1)} %bitcast.13, bf16[720,1440]{1,0:T(8,128)(2,1)} %bitcast.14), custom_call_target="tpu_custom_call" | custom-call | flops 16000000000 | bytes 7000000 | tf_op jit(solution)/shard_map/pallas_call | solution.py:368
  190.6 1.9 copy.22
  192.5 0.0 copy-done
  192.5 0.1 eq.27
  192.6 0.2 convert_reduce_fusion
  192.8 76.6 %psum.7 = s32[2,128]{1,0:T(2,128)S(1)} all-reduce(s32[2,128]{1,0:T(2,128)S(1)} %pad_add_fusion), channel_id=1, replica_groups=mesh['rep'=16,'exp'=16] {'rep','exp'}, use_global_device_ids=true, to_apply=%region_1.2 | all-reduce | flops 256 | bytes 2048 | tf_op jit(solution)/shard_map/psum | solution.py:402
  269.4 0.6 constant_dynamic-slice_fusion
  270.7 0.0 copy-done.1
  270.7 0.7 compare_reduce_fusion
  272.6 0.6 gather_fusion
  273.2 0.0 copy-done.2
  273.2 0.6 fusion
  (5 shorter events, 0.0 us)
Async XLA Ops:
  5.3 187.2 %copy-start = (s32[128,4]{1,0:T(8,128)S(1)}, s32[128,4]{1,0:T(8,128)}, u32[]{:S(2)}) copy-start(s32[128,4]{1,0:T(8,128)} %copy.18.ids_ref) | copy-start | bytes 6148
  5.3 265.3 %copy-start.1 = (s32[2]{0:T(128)S(1)}, s32[2]{0:T(128)}, u32[]{:S(2)}) copy-start(s32[2]{0:T(128)} %param.12) | copy-start | bytes 28
  5.3 267.9 %copy-start.2 = (s32[2]{0:T(128)S(1)}, s32[2]{0:T(128)}, u32[]{:S(2)}) copy-start(s32[2]{0:T(128)} %param.13) | copy-start | bytes 28
where the time goes:
time: 277 us; the launch traced here: 276 us
  Pallas kernels  185 us (67%)
  blocking collectives  76.6 us (28%)
  local copies, waits for them, and re-layouts  8 us (3%)
  between operations  4.3 us (2%)
    pallas_call x1, Pallas kernels, moe(): pl.pallas_call(moe_kernel, out_shape=jax.ShapeDtypeStruct((rows, model),...  185 us
    psum x1, blocking collectives, local(): both = lax.psum(jnp.stack([counts, upper]), ('rep', 'exp'))  76.6 us
    unnamed x10, local copies, waits for them, and re-layouts  6.64 us

commit v1 on v0

--- a/solution.py
+++ b/solution.py
@@ -24,9 +24,9 @@
     return (y * 4 + lax.rem(z, 2) * 2 + k, x * 4 + lax.div(z, 2))
 
 
-def moe_kernel(ids_ref, wts_ref, tok_ref, wi_hbm, wd_hbm, out_ref, *scratch):
+def moe_kernel(ids_ref, wts_ref, tok_ref, source_ref, host_ref, wi_hbm, wd_hbm, out_ref, load_ref, *scratch):
     T, G, XY, PP, RY, SS, RX, ZC, ZR = (scratch[i * NC:(i + 1) * NC] for i in range(9))
-    meta, OH, CT, WI, WU, WD, send_sems, recv_sems, meta_send, meta_recv, load_sems = scratch[9 * NC:]
+    meta, OH, CT, WI, WU, WD, CX, CY, CE, send_sems, recv_sems, meta_send, meta_recv, load_sems = scratch[9 * NC:]
     tok_rows = tok_ref.shape[0]
     half = tok_rows // 2
     ff = WD.shape[0]
@@ -79,7 +79,8 @@
         peer = lax.rem(me + j, NSRC)
         pl.semaphore_signal(barrier, inc=1, device_id=device(x, y, lax.div(peer, 2), lax.rem(peer, 2)), device_id_type=MESH)
     for j in range(1, NX):
-        pl.semaphore_signal(barrier, inc=1, device_id=device(xat(j), y, z, k), device_id_type=MESH)
+        for i in range(NZ // 2):
+            pl.semaphore_signal(barrier, inc=1, device_id=device(xat(j), y, zat(2 * i), k), device_id_type=MESH)
     for j in range(1, NY):
         pl.semaphore_signal(barrier, inc=1, device_id=device(x, yat(j), z, k), device_id_type=MESH)
 
@@ -89,7 +90,7 @@
     load_down.start()
     for c, (lo, hi) in enumerate(CHUNKS):
         T[c][me] = tok_ref[:, lo:hi]
-    pl.semaphore_wait(barrier, NSRC - 1 + NX - 1 + NY - 1)
+    pl.semaphore_wait(barrier, NSRC - 1 + (NX - 1) * (NZ // 2) + NY - 1)
 
     def block(c, d, rows=None, core=None):
         ref = T[c].at[zat(d) * 2 + (k if core is None else core)]
@@ -184,6 +185,55 @@
             CT[pl.ds(pl.multiple_of(s * tok_rows, tok_rows), tok_rows), :] = total.astype(BF16)
             return carry
         lax.fori_loop(0, NSRC, one, 0)
+
+    def count_pairs():
+        codes = meta[...] - (me * CODE).astype(F32)
+        valid = lax.broadcasted_iota(jnp.int32, codes.shape, 1) < 4
+        unit = lax.broadcasted_iota(jnp.int32, (8, 128), 0)
+        table = jnp.zeros((8, 128), F32)
+        for u in range(2 * NX):
+            inside = jnp.logical_and(valid, jnp.logical_and(codes >= u * UNIT, codes < (u + 1) * UNIT))
+            hits = jnp.sum(jnp.sum(jnp.where(inside, 1.0, 0.0), axis=0), axis=0, keepdims=True)
+            table = jnp.where(unit == u, hits, table)
+        CX[x] = table
+        for j in range(1, NX):
+            send(("cx", j), CX.at[x], CX.at[x], device(xat(j), y, z, k))
+
+    def count_along_y():
+        for j in range(1, NX):
+            arrived(("cx", j), CX.at[xat(-j)])
+        CY[y] = CX[0] + CX[1] + CX[2] + CX[3]
+        for j in range(1, NY):
+            send(("cy", j), CY.at[y], CY.at[y], device(x, yat(j), z, k))
+
+    def count_upper():
+        for j in range(1, NY):
+            arrived(("cy", j), CY.at[yat(-j)])
+        mine = lax.broadcasted_iota(jnp.int32, (8, 128), 0) == x * 2 + p
+        CE[NSRC] = jnp.where(mine, CY[0] + CY[1], 0.0)
+        CE[ex] = jnp.where(mine, CY[2] + CY[3], 0.0)
+        for i in range(NX):
+            for j in range(NZ // 2):
+                if i or j:
+                    send(("ce", i, j), CE.at[ex], CE.at[ex], device(xat(i), y, zat(2 * j), k))
+
+    def finish_load():
+        for i in range(NX):
+            for j in range(NZ // 2):
+                if i or j:
+                    column = xat(-i) * 4 + lax.div(zat(NZ - 2 * j), 2)
+                    arrived(("ce", i, j), CE.at[column])
+        total = CE[NSRC]
+        upper = CE[ex]
+        for h in range(source_ref.shape[0]):
+            upper = jnp.where(source_ref[h] == ex, 0.0, upper)
+        total = total + upper
+        for h in range(source_ref.shape[0]):
+            for i in range(NSRC):
+                taken = jnp.logical_and(host_ref[h] == ex, source_ref[h] == i)
+                total = total + jnp.where(taken, CE[i], 0.0)
+        summed = jnp.sum(jnp.sum(total, axis=0, keepdims=True), axis=1, keepdims=True)
+        load_ref[...] = summed.astype(jnp.int32)
 
     def x_stage(c):
         width = CHUNKS[c][1] - CHUNKS[c][0]
@@ -321,6 +371,7 @@
                 gather_step(c, s)
         if t == 3:
             build_pick()
+            count_pairs()
         for c in range(NC):
             if t - 2 * c == 5:
                 x_stage(c)
@@ -328,7 +379,9 @@
                     y_stage(c - 1)
         if t == 6:
             load_weights()
+            count_along_y()
     y_stage(NC - 1)
+    count_upper()
     expert(0)
     drain()
     build_combine()
@@ -337,6 +390,7 @@
         if j == 3:
             for c in range(NC):
                 halves(c, 1)
+    finish_load()
     for c in range(NC):
         halves(c, 0)
     order = sorted((s + 2 * c, -c, c, s) for c in range(NC) for s in range(5))
@@ -355,21 +409,22 @@
     assert len(ids_of) <= send_sems.shape[0]
 
 
-def moe(ids, weights, tokens, w_in, w_down):
+def moe(ids, weights, tokens, source, host, w_in, w_down):
     rows, model = tokens.shape
     widths = [hi - lo for lo, hi in CHUNKS]
     lead = (
         (NSRC, rows), (3, 2, UNIT), (5, NX, UNIT), (4, NX, UNIT), (3, NX, UNIT), (2, NX, UNIT), (NX, 2, UNIT),
         (NZ, rows), (8, rows))
     buffers = [pltpu.VMEM(shape + (width,), BF16) for shape in lead for width in widths]
-    copies = NC * (8 + 8 + 3 + 3 + 3 + 6 + 8 + 8)
+    copies = NC * (8 + 8 + 3 + 3 + 3 + 6 + 8 + 8) + 3 + 3 + 15
     vmem = pl.BlockSpec(memory_space=pltpu.VMEM)
+    smem = pl.BlockSpec(memory_space=pltpu.SMEM)
     hbm = pl.BlockSpec(memory_space=pl.ANY)
     return pl.pallas_call(
         moe_kernel,
-        out_shape=jax.ShapeDtypeStruct((rows, model), BF16),
-        in_specs=[vmem, vmem, vmem, hbm, hbm],
-        out_specs=vmem,
+        out_shape=(jax.ShapeDtypeStruct((rows, model), BF16), jax.ShapeDtypeStruct((1, 1), jnp.int32)),
+        in_specs=[vmem, vmem, vmem, smem, smem, hbm, hbm],
+        out_specs=(vmem, vmem),
         scratch_shapes=buffers + [
             pltpu.VMEM((NSRC, 8, 128), F32),
             pltpu.VMEM((ROWS, NSRC * rows), BF16),
@@ -377,6 +432,9 @@
             pltpu.VMEM(w_in.shape, BF16),
             pltpu.VMEM((w_in.shape[0], w_down.shape[0]), BF16),
             pltpu.VMEM(w_down.shape, BF16),
+            pltpu.VMEM((NX, 8, 128), F32),
+            pltpu.VMEM((NY, 8, 128), F32),
+            pltpu.VMEM((NSRC + 1, 8, 128), F32),
             pltpu.SemaphoreType.DMA((copies,)),
             pltpu.SemaphoreType.DMA((copies,)),
             pltpu.SemaphoreType.DMA((NSRC,)),
@@ -386,30 +444,11 @@
         compiler_params=pltpu.CompilerParams(
             collective_id=0, has_side_effects=True, vmem_limit_bytes=60 * 1024 * 1024),
         cost_estimate=pl.CostEstimate(flops=16 * 10**9, bytes_accessed=7 * 10**6, transcendentals=10**6),
-    )(ids, weights, tokens, w_in, w_down)
+    )(ids, weights, tokens, source, host, w_in, w_down)
 
 
 def local(tokens, expert_ids, route_weights, w_in, w_down, spare_source, spare_host):
-    rep_count = lax.axis_size("rep")
-    column_count = lax.axis_size("exp")
-    group_count = rep_count // 2
-    expert_count = group_count * column_count
-    rep, column = lax.axis_index("rep"), lax.axis_index("exp")
-
-    experts = jnp.arange(expert_count, dtype=jnp.int32)
-    counts = jnp.sum((expert_ids.reshape(-1)[:, None] == experts[None, :]).astype(jnp.int32), axis=0)
-    upper = jnp.where(rep >= group_count, counts, 0)
-    both = lax.psum(jnp.stack([counts, upper]), ("rep", "exp"))
-
-    mixed = moe(expert_ids, route_weights, tokens, w_in[0, 0], w_down[0, 0])
-
-    residue = rep % group_count
-    own = column * group_count + residue
-    is_source = jnp.any(column == spare_source)
-    load = jnp.take(both[0], own) - jnp.where(is_source, jnp.take(both[1], own), 0)
-    copied = jnp.take(both[1], spare_source * group_count + residue)
-    load = load + jnp.sum(jnp.where(column == spare_host, copied, 0))
-    return mixed, load.astype(jnp.int32).reshape(1, 1)
+    return moe(expert_ids, route_weights, tokens, spare_source, spare_host, w_in[0, 0], w_down[0, 0])
 
 
 def solution(mesh):

time: 277 us -> 201 us (0.73)
  blocking collectives: 76.6 us -> 0 us
  Pallas kernels: 185 us -> 191 us
    psum x1 -> x0, blocking collectives: 76.6 us -> none  [local(): both = lax.psum(jnp.stack([counts, upper]), ('rep', 'exp'))]
    pallas_call x1, Pallas kernels: 185 us -> 191 us  [moe(): pl.pallas_call(moe_kernel, out_shape=(jax.ShapeDtypeStruct((rows, model),...]
    unnamed x10 -> x3, local copies, waits for them, and re-layouts: 6.64 us -> 4.72 us
where the time goes in v1:
time: 201 us; the launch traced here: 200 us
  Pallas kernels  191 us (95%)
  local copies, waits for them, and re-layouts  6.64 us (3%)
  between operations  2.39 us (1%)
    pallas_call x1, Pallas kernels, moe(): pl.pallas_call(moe_kernel, out_shape=(jax.ShapeDtypeStruct((rows, model),...  191 us
    unnamed x3, local copies, waits for them, and re-layouts  4.72 us

profile of v1, /device:TPU:32, one launch (start us, length us, event | category | flops | bytes accessed | tf_op | source)
XLA Modules:
  0.0 200.2 jit_solution(10087823991192559939)
XLA Ops:
  0.6 1.4 copy.9.ids_ref
  2.0 1.4 copy.10.wts_ref
  3.5 1.9 copy.11.tok_ref
  5.4 191.2 %shard_map.86 = (bf16[128,1440]{1,0:T(8,128)(2,1)}, s32[1,1]{1,0:T(1,128)}) custom-call(s32[128,4]{1,0:T(8,128)} %copy.9.ids_ref, f32[128,4]{1,0:T(8,128)} %copy.10.wts_ref, bf16[128,1440]{1,0:T(8,128)(2,1)} %copy.11.tok_ref, s32[2]{0:T(128)} %source_ref.1, s32[2]{0:T(128)} %host_ref.1, bf16[1440,1440]{1,0:T(8,128)(2,1)} %bitcast.2, bf16[720,1440]{1,0:T(8,128)(2,1)} %bitcast.3), custom_call_target="tpu_custom_call" | custom-call | flops 16000000000 | bytes 7000000 | tf_op jit(solution)/shard_map/pallas_call | solution.py:423
  196.6 1.9 copy.12

commit v2 on v1

v2 whole, which is shorter than its diff:
```python
import jax
import jax.numpy as jnp
from jax import lax
from jax.experimental import pallas as pl
from jax.experimental.pallas import tpu as pltpu
from jax.sharding import PartitionSpec as P

MESH = pl.DeviceIdType.MESH
F32 = jnp.float32
BF16 = jnp.bfloat16

NX, NY, NZ = 4, 4, 8
NSRC = 2 * NZ
CAP = 5
UNIT = NSRC * CAP
ROWS = NX * 2 * UNIT
CODE = 1024
CHUNKS = ((0, 256), (256, 768), (768, 1280), (1280, 1440))
BEGIN = (0, 1, 3, 5)
NC = len(CHUNKS)
OFFS = (0, -1, 1, -2, 2, -3, 3, 4)


def device(x, y, z, k):
    return (y * 4 + lax.rem(z, 2) * 2 + k, x * 4 + lax.div(z, 2))


def moe_kernel(ids_ref, wts_ref, tok_ref, source_ref, host_ref, wi_hbm, wd_hbm, out_ref, load_ref, *scratch):
    T, G, XY, PP, RY, SS, RX, ZC, ZR, OWN = (scratch[i * NC:(i + 1) * NC] for i in range(10))
    meta, OH, CT, WI, WU, WD, HID, CX, CY, CE, send_sems, recv_sems, meta_send, meta_recv, load_sems = scratch[10 * NC:]
    tok_rows = tok_ref.shape[1]
    half = tok_rows // 2
    ff = WD.shape[0]

    rep, ex = lax.axis_index("rep"), lax.axis_index("exp")
    y, k = lax.div(rep, 4), lax.rem(rep, 2)
    x = lax.div(ex, 4)
    z = lax.rem(ex, 4) * 2 + lax.rem(lax.div(rep, 2), 2)
    me = k * NZ + z
    p = lax.rem(y, 2)

    def zat(d):
        return lax.rem(z + d + NZ, NZ)

    def yat(d):
        return lax.rem(y + d + NY, NY)

    def xat(d):
        return lax.rem(x + d + NX, NX)

    ids_of = {}
    sends = []

    def sem_of(name):
        if name not in ids_of:
            ids_of[name] = len(ids_of)
        return ids_of[name]

    def send(name, src, dst, to):
        i = sem_of(name)
        copy = pltpu.make_async_remote_copy(
            src_ref=src, dst_ref=dst, send_sem=send_sems.at[i], recv_sem=recv_sems.at[i],
            device_id=to, device_id_type=MESH)
        copy.start()
        sends.append(copy)

    def arrived(name, dst):
        i = sem_of(name)
        pltpu.make_async_remote_copy(
            src_ref=dst, dst_ref=dst, send_sem=send_sems.at[i], recv_sem=recv_sems.at[i],
            device_id=device(x, y, z, 1 - k), device_id_type=MESH).wait_recv()

    def drain():
        for copy in sends:
            copy.wait_send()
        sends.clear()

    barrier = pltpu.get_barrier_semaphore()
    for j in range(1, NSRC):
        peer = lax.rem(me + j, NSRC)
        pl.semaphore_signal(barrier, inc=1, device_id=device(x, y, lax.rem(peer, NZ), lax.div(peer, NZ)), device_id_type=MESH)
    for j in range(1, NX):
        pl.semaphore_signal(barrier, inc=1, device_id=device(xat(j), y, z, k), device_id_type=MESH)
    for j in range(1, NY):
        pl.semaphore_signal(barrier, inc=1, device_id=device(x, yat(j), z, k), device_id_type=MESH)

    load_in = pltpu.make_async_copy(wi_hbm, WI, load_sems.at[0])
    load_down = pltpu.make_async_copy(wd_hbm, WD, load_sems.at[1])
    load_in.start()
    load_down.start()
    for c, (lo, hi) in enumerate(CHUNKS):
        T[c][me] = tok_ref[lo:hi, :].T
    pl.semaphore_wait(barrier, NSRC - 1 + NX - 1 + NY - 1)

    def block(c, d, rows=None, core=None):
        ref = T[c].at[(k if core is None else core) * NZ + zat(d)]
        return ref if rows is None else ref.at[pl.ds(rows, half)]

    def to_sibling(c, d):
        send(("sib", c, d), block(c, d), block(c, d), device(x, y, z, 1 - k))

    def gather_step(c, s):
        if s == 1:
            to_send = ((1, block(c, 0)), (-1, block(c, 0)))
        else:
            for way in (1, -1):
                rows = None if s <= 4 else (0 if way == 1 else half)
                arrived(("ag", c, s - 1, way), block(c, -(s - 1) * way, rows))
            to_send = ()
            if s <= 4:
                to_send = tuple(
                    (way, block(c, -(s - 1) * way, None if s < 4 else (0 if way == 1 else half))) for way in (1, -1))
        for way, ref in to_send:
            send(("ag", c, s, way), ref, ref, device(x, y, zat(way), k))
        if s == 1:
            to_sibling(c, 0)
        elif s <= 4:
            to_sibling(c, -(s - 1))
            to_sibling(c, s - 1)
        else:
            to_sibling(c, 4)

    def make_meta():
        experts = lax.broadcasted_iota(jnp.int32, (128, tok_rows), 0)
        hits = [(ids_ref[i:i + 1, :] == experts).astype(F32) for i in range(4)]
        total = hits[0] + hits[1] + hits[2] + hits[3]
        before = (lax.broadcasted_iota(jnp.int32, (tok_rows, tok_rows), 0)
                  < lax.broadcasted_iota(jnp.int32, (tok_rows, tok_rows), 1)).astype(F32).astype(BF16)
        earlier = jnp.dot(total.astype(BF16), before, preferred_element_type=F32)
        for i in range(4):
            rank = jnp.sum(earlier * hits[i], axis=0, keepdims=True)
            e = ids_ref[i:i + 1, :]
            owner = (e & 1) * NZ + ((e >> 3) & 3) * 2 + ((e >> 1) & 1)
            place = ((e >> 5) * 2 + ((e >> 2) & 1)) * UNIT
            meta[me, i:i + 1, :] = (owner * CODE + place).astype(F32) + rank
            meta[me, 4 + i:5 + i, :] = wts_ref[i:i + 1, :]

    def send_meta():
        def one(j, carry):
            peer = lax.rem(me + j, NSRC)
            pltpu.make_async_remote_copy(
                src_ref=meta.at[me], dst_ref=meta.at[me], send_sem=meta_send.at[j], recv_sem=meta_recv.at[j],
                device_id=device(x, y, lax.rem(peer, NZ), lax.div(peer, NZ)), device_id_type=MESH).start()
            return carry
        lax.fori_loop(1, NSRC, one, 0)

    def meta_copy(j):
        peer = lax.rem(me + NSRC - j, NSRC)
        return pltpu.make_async_remote_copy(
            src_ref=meta.at[peer], dst_ref=meta.at[peer], send_sem=meta_send.at[j], recv_sem=meta_recv.at[j],
            device_id=device(x, y, lax.rem(peer, NZ), lax.div(peer, NZ)), device_id_type=MESH)

    def build_pick():
        def wait_one(j, carry):
            meta_copy(j).wait_recv()
            return carry
        lax.fori_loop(1, NSRC, wait_one, 0)

        def one(s, carry):
            row = lax.broadcasted_iota(jnp.int32, (ROWS, tok_rows), 0).astype(F32)
            shift = (s * CAP - me * CODE).astype(F32)
            codes = meta[s] + shift
            hit = row == codes[0:1, :]
            for i in range(1, 4):
                hit = jnp.logical_or(hit, row == codes[i:i + 1, :])
            OH[:, pl.ds(pl.multiple_of(s * tok_rows, tok_rows), tok_rows)] = jnp.where(hit, 1.0, 0.0).astype(BF16)
            return carry
        lax.fori_loop(0, NSRC, one, 0)

    def build_combine():
        def one(s, carry):
            col = lax.broadcasted_iota(jnp.int32, (tok_rows, ROWS), 1).astype(F32)
            shift = (s * CAP - me * CODE).astype(F32)
            info = meta[s].T
            total = jnp.zeros((tok_rows, ROWS), F32)
            for i in range(4):
                total = jnp.where(col == info[:, i:i + 1] + shift, info[:, 4 + i:5 + i], total)
            CT[pl.ds(pl.multiple_of(s * tok_rows, tok_rows), tok_rows), :] = total.astype(BF16)
            return carry
        lax.fori_loop(0, NSRC, one, 0)

    def count_pairs():
        codes = meta[...] - (me * CODE).astype(F32)
        valid = lax.broadcasted_iota(jnp.int32, codes.shape, 1) < 4
        unit = lax.broadcasted_iota(jnp.int32, (8, 128), 0)
        table = jnp.zeros((8, 128), F32)
        for u in range(2 * NX):
            inside = jnp.logical_and(valid, jnp.logical_and(codes >= u * UNIT, codes < (u + 1) * UNIT))
            hits = jnp.sum(jnp.sum(jnp.where(inside, 1.0, 0.0), axis=0), axis=0, keepdims=True)
            table = jnp.where(unit == u, hits, table)
        CX[x] = table
        for j in range(1, NX):
            send(("cx", j), CX.at[x], CX.at[x], device(xat(j), y, z, k))

    def count_along_y():
        for j in range(1, NX):
            arrived(("cx", j), CX.at[xat(-j)])
        CY[y] = CX[0] + CX[1] + CX[2] + CX[3]
        for j in range(1, NY):
            send(("cy", j), CY.at[y], CY.at[y], device(x, yat(j), z, k))

    def count_upper():
        for j in range(1, NY):
            arrived(("cy", j), CY.at[yat(-j)])
        mine = lax.broadcasted_iota(jnp.int32, (8, 128), 0) == x * 2 + p
        CE[NSRC] = jnp.where(mine, CY[0] + CY[1], 0.0)
        CE[ex] = jnp.where(mine, CY[2] + CY[3], 0.0)
        for j in range(1, NX):
            send(("ce", j), CE.at[ex], CE.at[ex], device(xat(j), y, z, k))

    def column(i, j):
        return i * 4 + lax.div(zat(NZ - 2 * j), 2)

    def spread_upper():
        for j in range(1, NX):
            arrived(("ce", j), CE.at[xat(-j) * 4 + lax.div(z, 2)])
        for j in range(1, NZ // 2):
            for i in range(NX):
                send(("cz", i, j), CE.at[column(i, 0)], CE.at[column(i, 0)], device(x, y, zat(2 * j), k))

    def finish_load():
        for j in range(1, NZ // 2):
            for i in range(NX):
                arrived(("cz", i, j), CE.at[column(i, j)])
        total = CE[NSRC]
        upper = CE[ex]
        for h in range(source_ref.shape[0]):
            upper = jnp.where(source_ref[h] == ex, 0.0, upper)
        total = total + upper
        for h in range(source_ref.shape[0]):
            for i in range(NSRC):
                taken = jnp.logical_and(host_ref[h] == ex, source_ref[h] == i)
                total = total + jnp.where(taken, CE[i], 0.0)
        summed = jnp.sum(jnp.sum(total, axis=0, keepdims=True), axis=1, keepdims=True)
        load_ref[...] = summed.astype(jnp.int32)

    def x_stage(c):
        width = CHUNKS[c][1] - CHUNKS[c][0]
        for d in OFFS:
            arrived(("sib", c, d), block(c, d, core=1 - k))
        picked = jnp.dot(OH[...], T[c][...].reshape(NSRC * tok_rows, width), preferred_element_type=F32)
        G[c][...] = picked.astype(BF16).reshape(NX, 2, UNIT, width)
        for j in (2, 1, 3):
            xp = xat(j)
            send(("x", c, j), G[c].at[xp], XY[c].at[pl.ds(0, 2), x], device(xp, y, z, k))
        XY[c][0, x] = G[c][x, 0]
        XY[c][1, x] = G[c][x, 1]

    def y_stage(c):
        for j in (1, 3, 2):
            arrived(("x", c, j), XY[c].at[pl.ds(0, 2), xat(-j)])
        for j in (1, 3, 2):
            a = lax.rem(p + j, 2)
            send(("y", c, j), XY[c].at[a], XY[c].at[1 + j], device(x, yat(j), z, k))

    def load_weights():
        load_in.wait()
        load_down.wait()

        def one(i, carry):
            rows = pl.ds(pl.multiple_of(i * 160, 16), 160)
            WU[rows, :] = WI[rows, ff:2 * ff]
            return carry
        lax.fori_loop(0, WI.shape[0] // 160, one, 0)

    def expert(j):
        slot = p if j == 0 else 1 + j
        gate = up = None
        for c, (lo, hi) in enumerate(CHUNKS):
            if j:
                arrived(("y", c, j), XY[c].at[slot])
            rows = XY[c][slot].reshape(NX * UNIT, hi - lo)
            g = jnp.dot(rows, WI[lo:hi, 0:ff], preferred_element_type=F32)
            u = jnp.dot(rows, WU[lo:hi, :], preferred_element_type=F32)
            gate, up = (g, u) if gate is None else (gate + g, up + u)
        HID[j * NX * UNIT:(j + 1) * NX * UNIT, :] = ((up + 1.0) * gate * jax.nn.sigmoid(1.702 * gate)).astype(BF16)

    def down(c):
        lo, hi = CHUNKS[c]
        part = jnp.dot(HID[...], WD[:, lo:hi], preferred_element_type=F32).astype(BF16)
        PP[c][...] = part.reshape(NY, NX, UNIT, hi - lo)
        for j in (1, 3, 2):
            send(("ry", c, j), PP[c].at[j], RY[c].at[j - 1], device(x, yat(-j), z, k))

    def halves(c):
        for j in (1, 3, 2):
            arrived(("ry", c, j), RY[c].at[j - 1])

        def one(i, carry):
            SS[c][p, i] = (PP[c][0, i].astype(F32) + RY[c][1, i].astype(F32)).astype(BF16)
            SS[c][1 - p, i] = (RY[c][0, i].astype(F32) + RY[c][2, i].astype(F32)).astype(BF16)
            return carry
        lax.fori_loop(0, NX, one, 0)
        for j in (2, 1, 3):
            xs = xat(j)
            send(("rx", c, j), SS[c].at[pl.ds(0, 2), xs], RX[c].at[x], device(xs, y, z, k))
        RX[c][x, 0] = SS[c][0, x]
        RX[c][x, 1] = SS[c][1, x]

    def combine(c):
        lo, hi = CHUNKS[c]
        for j in (2, 1, 3):
            arrived(("rx", c, j), RX[c].at[xat(-j)])

        def all_rows(core):
            rows = CT[pl.ds(pl.multiple_of(core * NZ * tok_rows, tok_rows), NZ * tok_rows), :]
            total = jnp.dot(rows, RX[c][...].reshape(ROWS, hi - lo), preferred_element_type=F32)
            return total.reshape(NZ, tok_rows, hi - lo)
        other = pl.ds((1 - k) * NZ, NZ)
        T[c][other] = all_rows(1 - k).astype(BF16)
        send(("zc", c), T[c].at[other], ZC[c], device(x, y, z, 1 - k))
        OWN[c][...] = all_rows(k)

    def scatter_step(c, s):
        lo, hi = CHUNKS[c]
        if s == 0:
            arrived(("zc", c), ZC[c])

        def partial(d, rows=slice(None)):
            return OWN[c][zat(d), rows] + ZC[c][zat(d), rows].astype(F32)

        if s == 0:
            own = T[c].at[k * NZ + zat(4)]
            own[...] = partial(4).astype(BF16)
            for i, way in enumerate((1, -1)):
                rows = pl.ds(i * half, half)
                send(("rs", c, 0, way), own.at[rows], ZR[c].at[i * 4, rows], device(x, y, zat(way), k))
        elif s < 4:
            for i, way in enumerate((1, -1)):
                d = way * (4 - s)
                own = T[c].at[k * NZ + zat(d)]
                if s == 1:
                    rows = pl.ds(i * half, half)
                    rest = pl.ds((1 - i) * half, half)
                    own[rest, :] = partial(d, rest).astype(BF16)
                    arrived(("rs", c, 0, way), ZR[c].at[i * 4, rows])
                    own[rows, :] = (partial(d, rows) + ZR[c][i * 4, rows].astype(F32)).astype(BF16)
                else:
                    arrived(("rs", c, s - 1, way), ZR[c].at[i * 4 + s - 1])
                    own[...] = (partial(d) + ZR[c][i * 4 + s - 1].astype(F32)).astype(BF16)
                send(("rs", c, s, way), own, ZR[c].at[i * 4 + s], device(x, y, zat(way), k))
        else:
            total = partial(0)
            for i, way in enumerate((1, -1)):
                arrived(("rs", c, 3, way), ZR[c].at[i * 4 + 3])
                total = total + ZR[c][i * 4 + 3].astype(F32)
            out_ref[lo:hi, :] = total.T.astype(BF16)

    gather_step(0, 1)
    make_meta()
    send_meta()
    waiting = []
    for t in range(2, 6 + BEGIN[-1]):
        for c in range(NC):
            s = t - BEGIN[c]
            if 1 <= s <= 5:
                gather_step(c, s)
        if t == 3:
            build_pick()
        while waiting:
            y_stage(waiting.pop())
        for c in range(NC):
            if t - BEGIN[c] == 5:
                x_stage(c)
                waiting.append(c)
                if c == 0:
                    count_pairs()
                    load_weights()
                if c == 2:
                    count_along_y()
    y_stage(NC - 1)
    count_upper()
    expert(0)
    build_combine()
    drain()
    spread_upper()
    for j in (1, 3, 2):
        expert(j)
    down(0)
    down(1)
    halves(0)
    down(2)
    combine(0)
    scatter_step(0, 0)
    halves(1)
    down(3)
    finish_load()
    scatter_step(0, 1)
    combine(1)
    scatter_step(1, 0)
    scatter_step(0, 2)
    halves(2)
    scatter_step(1, 1)
    scatter_step(0, 3)
    combine(2)
    scatter_step(2, 0)
    scatter_step(1, 2)
    scatter_step(0, 4)
    halves(3)
    scatter_step(2, 1)
    scatter_step(1, 3)
    combine(3)
    scatter_step(3, 0)
    scatter_step(2, 2)
    scatter_step(3, 1)
    scatter_step(1, 4)
    scatter_step(2, 3)
    scatter_step(3, 2)
    scatter_step(2, 4)
    scatter_step(3, 3)
    scatter_step(3, 4)
    drain()

    def end_one(j, carry):
        meta_copy(j).wait_send()
        return carry
    lax.fori_loop(1, NSRC, end_one, 0)
    assert len(ids_of) <= send_sems.shape[0]


def moe(ids, weights, tokens, source, host, w_in, w_down):
    model, rows = tokens.shape
    widths = [hi - lo for lo, hi in CHUNKS]
    lead = (
        (NSRC, rows), (NX, 2, UNIT), (5, NX, UNIT), (4, NX, UNIT), (3, NX, UNIT), (2, NX, UNIT), (NX, 2, UNIT),
        (NZ, rows), (8, rows))
    buffers = [pltpu.VMEM(shape + (width,), BF16) for shape in lead for width in widths]
    buffers += [pltpu.VMEM((NZ, rows, width), F32) for width in widths]
    copies = NC * (8 + 8 + 3 + 3 + 3 + 3 + 1 + 8) + 3 + 3 + 3 + 12
    vmem = pl.BlockSpec(memory_space=pltpu.VMEM)
    smem = pl.BlockSpec(memory_space=pltpu.SMEM)
    hbm = pl.BlockSpec(memory_space=pl.ANY)
    return pl.pallas_call(
        moe_kernel,
        out_shape=(jax.ShapeDtypeStruct((model, rows), BF16), jax.ShapeDtypeStruct((1, 1), jnp.int32)),
        in_specs=[vmem, vmem, vmem, smem, smem, hbm, hbm],
        out_specs=(vmem, vmem),
        scratch_shapes=buffers + [
            pltpu.VMEM((NSRC, 8, 128), F32),
            pltpu.VMEM((ROWS, NSRC * rows), BF16),
            pltpu.VMEM((NSRC * rows, ROWS), BF16),
            pltpu.VMEM(w_in.shape, BF16),
            pltpu.VMEM((w_in.shape[0], w_down.shape[0]), BF16),
            pltpu.VMEM(w_down.shape, BF16),
            pltpu.VMEM((NY * NX * UNIT, w_down.shape[0]), BF16),
            pltpu.VMEM((NX, 8, 128), F32),
            pltpu.VMEM((NY, 8, 128), F32),
            pltpu.VMEM((NSRC + 1, 8, 128), F32),
            pltpu.SemaphoreType.DMA((copies,)),
            pltpu.SemaphoreType.DMA((copies,)),
            pltpu.SemaphoreType.DMA((NSRC,)),
            pltpu.SemaphoreType.DMA((NSRC,)),
            pltpu.SemaphoreType.DMA((2,)),
        ],
        compiler_params=pltpu.CompilerParams(
            collective_id=0, has_side_effects=True, vmem_limit_bytes=60 * 1024 * 1024),
        cost_estimate=pl.CostEstimate(flops=16 * 10**9, bytes_accessed=7 * 10**6, transcendentals=10**6),
    )(ids, weights, tokens, source, host, w_in, w_down)


def local(tokens, expert_ids, route_weights, w_in, w_down, spare_source, spare_host):
    mixed, slot_load = moe(expert_ids.T, route_weights.T, tokens.T, spare_source, spare_host, w_in[0, 0], w_down[0, 0])
    return mixed.T, slot_load


def solution(mesh):
    placed = (
        P(("rep", "exp"), None),
        P(("rep", "exp"), None),
        P(("rep", "exp"), None),
        P("rep", "exp", None, None),
        P("rep", "exp", None, None),
        P(),
        P(),
    )
    return jax.shard_map(
        local,
        mesh=mesh,
        in_specs=placed,
        out_specs=(P(("rep", "exp"), None), P("rep", "exp")),
        check_vma=False,
    )
```

time: 201 us -> 173 us (0.86)
  Pallas kernels: 191 us -> 168 us
  local copies, waits for them, and re-layouts: 6.64 us -> 1.75 us
    pallas_call x1, Pallas kernels: 191 us -> 168 us  [moe(): pl.pallas_call(moe_kernel, out_shape=(jax.ShapeDtypeStruct((model, rows),...]
    unnamed x3 -> x1, local copies, waits for them, and re-layouts: 4.72 us -> 1.75 us
where the time goes in v2:
time: 173 us; the launch traced here: 172 us
  Pallas kernels  168 us (97%)
  between operations  2.39 us (1%)
  local copies, waits for them, and re-layouts  1.75 us (1%)
    pallas_call x1, Pallas kernels, moe(): pl.pallas_call(moe_kernel, out_shape=(jax.ShapeDtypeStruct((model, rows),...  168 us

profile of v2, /device:TPU:32, one launch (start us, length us, event | category | flops | bytes accessed | tf_op | source)
XLA Modules:
  0.0 171.7 jit_solution(2812233040429816382)
XLA Ops:
  0.6 167.6 %shard_map.86 = (bf16[1440,128]{1,0:T(8,128)(2,1)}, s32[1,1]{1,0:T(1,128)}) custom-call(s32[4,128]{1,0:T(4,128)} %bitcast.10, f32[4,128]{1,0:T(4,128)} %bitcast.11, bf16[1440,128]{1,0:T(8,128)(2,1)} %bitcast.9, s32[2]{0:T(128)} %source_ref.1, s32[2]{0:T(128)} %host_ref.1, bf16[1440,1440]{1,0:T(8,128)(2,1)} %bitcast.7, bf16[720,1440]{1,0:T(8,128)(2,1)} %bitcast.8), custom_call_target="tpu_custom_call" | custom-call | flops 16000000000 | bytes 7000000 | tf_op jit(solution)/shard_map/pallas_call | solution.py:433
  168.2 1.7 %copy.11 = bf16[128,1440]{0,1:T(8,128)(2,1)} copy(bf16[128,1440]{0,1:T(8,128)(2,1)} %bitcast.6) | data formatting | bytes 737280

commit v3 on v2

--- a/solution.py
+++ b/solution.py
@@ -16,7 +16,9 @@
 ROWS = NX * 2 * UNIT
 CODE = 1024
 CHUNKS = ((0, 256), (256, 768), (768, 1280), (1280, 1440))
-BEGIN = (0, 1, 3, 5)
+BEGIN = (0, 2, 3, 1)
+OUTWARD = (0, 3, 1, 2)
+BACK = (0, 1, 2, 3)
 NC = len(CHUNKS)
 OFFS = (0, -1, 1, -2, 2, -3, 3, 4)
 
@@ -350,25 +352,24 @@
     make_meta()
     send_meta()
     waiting = []
-    for t in range(2, 6 + BEGIN[-1]):
-        for c in range(NC):
-            s = t - BEGIN[c]
-            if 1 <= s <= 5:
-                gather_step(c, s)
+    for t in range(2, 6 + max(BEGIN)):
+        for c in OUTWARD:
+            if 1 <= t - BEGIN[c] <= 5:
+                gather_step(c, t - BEGIN[c])
         if t == 3:
             build_pick()
         while waiting:
-            y_stage(waiting.pop())
-        for c in range(NC):
+            y_stage(waiting.pop(0))
+        for c in OUTWARD:
             if t - BEGIN[c] == 5:
                 x_stage(c)
                 waiting.append(c)
-                if c == 0:
+                if c == OUTWARD[0]:
                     count_pairs()
                     load_weights()
-                if c == 2:
+                if c == OUTWARD[2]:
                     count_along_y()
-    y_stage(NC - 1)
+    y_stage(waiting.pop(0))
     count_upper()
     expert(0)
     build_combine()
@@ -376,39 +377,39 @@
     spread_upper()
     for j in (1, 3, 2):
         expert(j)
-    down(0)
-    down(1)
-    halves(0)
-    down(2)
-    combine(0)
-    scatter_step(0, 0)
-    halves(1)
-    down(3)
+    down(BACK[0])
+    down(BACK[1])
+    halves(BACK[0])
+    down(BACK[2])
+    combine(BACK[0])
+    scatter_step(BACK[0], 0)
+    halves(BACK[1])
+    down(BACK[3])
     finish_load()
-    scatter_step(0, 1)
-    combine(1)
-    scatter_step(1, 0)
-    scatter_step(0, 2)
-    halves(2)
-    scatter_step(1, 1)
-    scatter_step(0, 3)
-    combine(2)
-    scatter_step(2, 0)
-    scatter_step(1, 2)
-    scatter_step(0, 4)
-    halves(3)
-    scatter_step(2, 1)
-    scatter_step(1, 3)
-    combine(3)
-    scatter_step(3, 0)
-    scatter_step(2, 2)
-    scatter_step(3, 1)
-    scatter_step(1, 4)
-    scatter_step(2, 3)
-    scatter_step(3, 2)
-    scatter_step(2, 4)
-    scatter_step(3, 3)
-    scatter_step(3, 4)
+    scatter_step(BACK[0], 1)
+    combine(BACK[1])
+    scatter_step(BACK[1], 0)
+    scatter_step(BACK[0], 2)
+    halves(BACK[2])
+    scatter_step(BACK[1], 1)
+    scatter_step(BACK[0], 3)
+    combine(BACK[2])
+    scatter_step(BACK[2], 0)
+    scatter_step(BACK[1], 2)
+    scatter_step(BACK[0], 4)
+    halves(BACK[3])
+    scatter_step(BACK[2], 1)
+    scatter_step(BACK[1], 3)
+    combine(BACK[3])
+    scatter_step(BACK[3], 0)
+    scatter_step(BACK[2], 2)
+    scatter_step(BACK[3], 1)
+    scatter_step(BACK[1], 4)
+    scatter_step(BACK[2], 3)
+    scatter_step(BACK[3], 2)
+    scatter_step(BACK[2], 4)
+    scatter_step(BACK[3], 3)
+    scatter_step(BACK[3], 4)
     drain()
 
     def end_one(j, carry):

time: 173 us -> 171 us (0.988)
  no operation moved by 1% of the time
where the time goes in v3:
time: 171 us
  Pallas kernels  167 us (98%)
  between operations  2.39 us (1%)
  local copies, waits for them, and re-layouts  1.75 us (1%)
    pallas_call x1, Pallas kernels, moe(): pl.pallas_call(moe_kernel, out_shape=(jax.ShapeDtypeStruct((model, rows),...  167 us

profile of v3, /device:TPU:32, one launch (start us, length us, event | category | flops | bytes accessed | tf_op | source)
XLA Modules:
  0.0 170.8 jit_solution(15719170460914570024)
XLA Ops:
  0.6 166.6 %shard_map.86 = (bf16[1440,128]{1,0:T(8,128)(2,1)}, s32[1,1]{1,0:T(1,128)}) custom-call(s32[4,128]{1,0:T(4,128)} %bitcast.10, f32[4,128]{1,0:T(4,128)} %bitcast.11, bf16[1440,128]{1,0:T(8,128)(2,1)} %bitcast.9, s32[2]{0:T(128)} %source_ref.1, s32[2]{0:T(128)} %host_ref.1, bf16[1440,1440]{1,0:T(8,128)(2,1)} %bitcast.7, bf16[720,1440]{1,0:T(8,128)(2,1)} %bitcast.8), custom_call_target="tpu_custom_call" | custom-call | flops 16000000000 | bytes 7000000 | tf_op jit(solution)/shard_map/pallas_call | solution.py:434
  167.3 1.7 %copy.11 = bf16[128,1440]{0,1:T(8,128)(2,1)} copy(bf16[128,1440]{0,1:T(8,128)(2,1)} %bitcast.6) | data formatting | bytes 737280

commit v4 on v3

--- a/solution.py
+++ b/solution.py
@@ -29,7 +29,7 @@
 
 def moe_kernel(ids_ref, wts_ref, tok_ref, source_ref, host_ref, wi_hbm, wd_hbm, out_ref, load_ref, *scratch):
     T, G, XY, PP, RY, SS, RX, ZC, ZR, OWN = (scratch[i * NC:(i + 1) * NC] for i in range(10))
-    meta, OH, CT, WI, WU, WD, HID, CX, CY, CE, send_sems, recv_sems, meta_send, meta_recv, load_sems = scratch[10 * NC:]
+    meta, OH, CT, WI, WU, WD, HID, ACC, CX, CY, CE, send_sems, recv_sems, meta_send, meta_recv, load_sems = scratch[10 * NC:]
     tok_rows = tok_ref.shape[1]
     half = tok_rows // 2
     ff = WD.shape[0]
@@ -265,17 +265,22 @@
             return carry
         lax.fori_loop(0, WI.shape[0] // 160, one, 0)
 
-    def expert(j):
+    def expert(j, chunks, first, last):
         slot = p if j == 0 else 1 + j
-        gate = up = None
-        for c, (lo, hi) in enumerate(CHUNKS):
+        gate, up = (None, None) if first else (ACC[j - 1, :, 0:ff], ACC[j - 1, :, 768:768 + ff])
+        for c in chunks:
+            lo, hi = CHUNKS[c]
             if j:
                 arrived(("y", c, j), XY[c].at[slot])
             rows = XY[c][slot].reshape(NX * UNIT, hi - lo)
             g = jnp.dot(rows, WI[lo:hi, 0:ff], preferred_element_type=F32)
             u = jnp.dot(rows, WU[lo:hi, :], preferred_element_type=F32)
             gate, up = (g, u) if gate is None else (gate + g, up + u)
-        HID[j * NX * UNIT:(j + 1) * NX * UNIT, :] = ((up + 1.0) * gate * jax.nn.sigmoid(1.702 * gate)).astype(BF16)
+        if last:
+            HID[j * NX * UNIT:(j + 1) * NX * UNIT, :] = ((up + 1.0) * gate * jax.nn.sigmoid(1.702 * gate)).astype(BF16)
+        else:
+            ACC[j - 1, :, 0:ff] = gate
+            ACC[j - 1, :, 768:768 + ff] = up
 
     def down(c):
         lo, hi = CHUNKS[c]
@@ -371,12 +376,14 @@
                     count_along_y()
     y_stage(waiting.pop(0))
     count_upper()
-    expert(0)
+    expert(0, OUTWARD, True, True)
     build_combine()
     drain()
     spread_upper()
     for j in (1, 3, 2):
-        expert(j)
+        expert(j, OUTWARD[:-1], True, False)
+    for j in (1, 3, 2):
+        expert(j, OUTWARD[-1:], False, True)
     down(BACK[0])
     down(BACK[1])
     halves(BACK[0])
@@ -444,6 +451,7 @@
             pltpu.VMEM((w_in.shape[0], w_down.shape[0]), BF16),
             pltpu.VMEM(w_down.shape, BF16),
             pltpu.VMEM((NY * NX * UNIT, w_down.shape[0]), BF16),
+            pltpu.VMEM((NY - 1, NX * UNIT, 1536), F32),
             pltpu.VMEM((NX, 8, 128), F32),
             pltpu.VMEM((NY, 8, 128), F32),
             pltpu.VMEM((NSRC + 1, 8, 128), F32),
@@ -454,7 +462,7 @@
             pltpu.SemaphoreType.DMA((2,)),
         ],
         compiler_params=pltpu.CompilerParams(
-            collective_id=0, has_side_effects=True, vmem_limit_bytes=60 * 1024 * 1024),
+            collective_id=0, has_side_effects=True, vmem_limit_bytes=62 * 1024 * 1024),
         cost_estimate=pl.CostEstimate(flops=16 * 10**9, bytes_accessed=7 * 10**6, transcendentals=10**6),
     )(ids, weights, tokens, source, host, w_in, w_down)
 

time: 171 us -> 172 us (level)
  no operation moved by 1% of the time
where the time goes in v4:
time: 172 us
  Pallas kernels  167 us (97%)
  between operations  2.39 us (1%)
  local copies, waits for them, and re-layouts  1.75 us (1%)
    pallas_call x1, Pallas kernels, moe(): pl.pallas_call(moe_kernel, out_shape=(jax.ShapeDtypeStruct((model, rows),...  167 us

profile of v4, /device:TPU:32, one launch (start us, length us, event | category | flops | bytes accessed | tf_op | source)
XLA Modules:
  0.0 171.6 jit_solution(14415779515594890775)
XLA Ops:
  0.6 167.4 %shard_map.86 = (bf16[1440,128]{1,0:T(8,128)(2,1)}, s32[1,1]{1,0:T(1,128)}) custom-call(s32[4,128]{1,0:T(4,128)} %bitcast.10, f32[4,128]{1,0:T(4,128)} %bitcast.11, bf16[1440,128]{1,0:T(8,128)(2,1)} %bitcast.9, s32[2]{0:T(128)} %source_ref.1, s32[2]{0:T(128)} %host_ref.1, bf16[1440,1440]{1,0:T(8,128)(2,1)} %bitcast.7, bf16[720,1440]{1,0:T(8,128)(2,1)} %bitcast.8), custom_call_target="tpu_custom_call" | custom-call | flops 16000000000 | bytes 7000000 | tf_op jit(solution)/shard_map/pallas_call | solution.py:441
  168.1 1.7 %copy.11 = bf16[128,1440]{0,1:T(8,128)(2,1)} copy(bf16[128,1440]{0,1:T(8,128)(2,1)} %bitcast.6) | data formatting | bytes 737280
